TPU v7x, 512 devices: a whole 4x4x16 slice. The times are simulated.
512 devices in a mesh: dp: 64 (over z, x), tensor: 8 (over y, core).
Axes of the slice: x: 4, y: 4, z: 16, core: 2. Of those that a mesh axis runs over, the one named last changes fastest.
Arguments:
- grad_out: bfloat16 [32768, 4096], P(('dp', 'tensor')), as said below
- attn_out: bfloat16 [32768, 2048], P('dp', 'tensor'), as said below
Outputs:
- combined: bfloat16 [4096, 2048], P('dp', 'tensor')
Inputs may be any that keep to these rules, and one draw needn't show every extreme that they name: `grad_out`: finite real values. `attn_out`: finite real values.
All inputs are finite; a program needn't handle non-finite values.
Results may differ from a plain program's by a relative error of at most 0.006.
Values may be sent and summed in bfloat16 or wider, within the bound.
A program may use at most 64 MiB of HBM per device.

v0:
```python
import jax
import jax.numpy as jnp
from jax import lax
from jax.sharding import PartitionSpec as P


def partner(block, axis, apart):
    count = lax.axis_size(axis)
    route = []
    for low in range(count):
        high = low | 1 << apart
        if high != low and high < count:
            route += [(low, high), (high, low)]
    return lax.ppermute(block, axis, route)


def shards(grad_out, attn_out):
    model_cols = grad_out.shape[1]
    head_cols = attn_out.shape[1]
    grad_local = lax.dot_general(
        lax.all_gather(grad_out, "tensor", axis=0, tiled=True),
        attn_out,
        (((0,), (0,)), ((), ())),
        preferred_element_type=jnp.float32,
    ).astype(jnp.bfloat16)
    replicas = lax.axis_size("dp")
    levels = replicas.bit_length() - 1
    my_index = lax.axis_index("dp")
    block_rows = model_cols // replicas
    held_blocks = grad_local.reshape(replicas, block_rows, head_cols)
    for section_index in range(levels):
        my_bit = my_index >> section_index & 1
        is_high = my_bit == 1
        block_count = held_blocks.shape[0]
        paired = held_blocks.reshape(block_count // 2, 2, block_rows, head_cols)
        lower_half = paired[:, 0]
        upper_half = paired[:, 1]
        kept_half = jnp.where(is_high, upper_half, lower_half)
        outgoing = jnp.where(is_high, lower_half, upper_half)
        arrived = partner(outgoing, "dp", section_index)
        first_f = jnp.where(is_high, arrived, kept_half).astype(jnp.float32)
        second_f = jnp.where(is_high, kept_half, arrived).astype(jnp.float32)
        partial_value = jnp.stack(
            [jnp.sum(first_f * second_f), jnp.sum(first_f * first_f), jnp.sum(second_f * second_f)]
        )
        summed = lax.psum(partial_value, "tensor")
        for inner_bit in range(section_index + 1):
            summed = summed + partner(summed, "dp", inner_bit)
        first_coef = 1.0 - summed[0] / (2.0 * (summed[1] + 1e-06))
        second_coef = 1.0 - summed[0] / (2.0 * (summed[2] + 1e-06))
        held_blocks = (first_coef * first_f + second_coef * second_f).astype(jnp.bfloat16)
    return held_blocks.reshape(block_rows, head_cols)


def solution(mesh):
    return jax.shard_map(
        shards,
        mesh=mesh,
        in_specs=(P(("dp", "tensor"), None), P("dp", "tensor")),
        out_specs=P("dp", "tensor"),
        check_vma=False,
    )
```

profile of v0, /device:TPU:1, one launch (start us, length us, event | category | flops | bytes accessed | tf_op | source)
XLA Modules:
  0.0 402.5 jit_solution(5946064257417146808)
XLA Ops:
  7.3 47.8 %all-gather.2.cloned.1.call-done = bf16[512,4096]{1,0:T(8,128)(2,1)} async-done(((bf16[64,4096]{1,0:T(8,128)(2,1)}), bf16[512,4096]{1,0:T(8,128)(2,1)}) %all-gather.2.cloned.1.call-update) | async-done | bytes 4194320 | tf_op jit(solution)/shard_map/all_gather | solution.py:21
  61.8 23.4 %collective-permute-done = bf16[32,64,256]{2,1,0:T(8,128)(2,1)} collective-permute-done((bf16[32,64,256]{2,1,0:T(8,128)(2,1)S(1)}, bf16[32,64,256]{2,1,0:T(8,128)(2,1)}, u32[]{:S(2)}, u32[]{:S(2)}) %collective-permute-start) | collective-permute-done | bytes 1048608 | tf_op jit(solution)/shard_map/ppermute | solution.py:14
  90.9 12.8 %psum.42 = f32[3]{0:T(128)S(1)} all-reduce(f32[3]{0:T(128)S(1)} %pad_maximum_fusion), channel_id=1, replica_groups=mesh['dp'=64,'tensor'=8] {'tensor'}, use_global_device_ids=true, to_apply=%region_3.4 | all-reduce | flops 3 | bytes 24 | tf_op jit(solution)/shard_map/psum | solution.py:46
  112.8 4.6 %collective-permute-start.2 = (bf16[16,64,256]{2,1,0:T(8,128)(2,1)S(1)}, bf16[16,64,256]{2,1,0:T(8,128)(2,1)S(1)}, u32[]{:S(2)}, u32[]{:S(2)}) collective-permute-start(bf16[16,64,256]{2,1,0:T(8,128)(2,1)S(1)} %fusion.16), channel_id=1, source_target_pairs={{0,16},{16,0},{8,24},{24,8},{32,48},{48,32},{40,56},{56,40},{64,80... | collective-permute-start | bytes 1572872 | tf_op jit(solution)/shard_map/ppermute | solution.py:14
  117.4 10.4 %collective-permute-done.2 = bf16[16,64,256]{2,1,0:T(8,128)(2,1)S(1)} collective-permute-done((bf16[16,64,256]{2,1,0:T(8,128)(2,1)S(1)}, bf16[16,64,256]{2,1,0:T(8,128)(2,1)S(1)}, u32[]{:S(2)}, u32[]{:S(2)}) %collective-permute-start.2) | collective-permute-done | bytes 524320 | tf_op jit(solution)/shard_map/ppermute | solution.py:14
  131.1 14.5 %psum.43 = f32[3]{0:T(128)S(1)} all-reduce(f32[3]{0:T(128)S(1)} %pad_maximum_fusion.1), channel_id=1, replica_groups=mesh['dp'=64,'tensor'=8] {'tensor'}, use_global_device_ids=true, to_apply=%region_7.8 | all-reduce | flops 3 | bytes 24 | tf_op jit(solution)/shard_map/psum | solution.py:46
  149.8 4.6 %collective-permute-start.4 = (f32[3]{0:T(128)S(1)}, f32[3]{0:T(128)S(1)}, u32[]{:S(2)}, u32[]{:S(2)}) collective-permute-start(f32[3]{0:T(128)S(1)} %add.145), channel_id=1, source_target_pairs={{0,16},{16,0},{8,24},{24,8},{32,48},{48,32},{40,56},{56,40},{64,80... | collective-permute-start | bytes 44 | tf_op jit(solution)/shard_map/ppermute | solution.py:14
  162.2 3.9 collective-permute-done.5
  169.0 15.9 %psum.44 = f32[3]{0:T(128)S(1)} all-reduce(f32[3]{0:T(128)S(1)} %pad_maximum_fusion.2), channel_id=1, replica_groups=mesh['dp'=64,'tensor'=8] {'tensor'}, use_global_device_ids=true, to_apply=%region_11.12 | all-reduce | flops 3 | bytes 24 | tf_op jit(solution)/shard_map/psum | solution.py:46
  189.2 4.6 %collective-permute-start.7 = (f32[3]{0:T(128)S(1)}, f32[3]{0:T(128)S(1)}, u32[]{:S(2)}, u32[]{:S(2)}) collective-permute-start(f32[3]{0:T(128)S(1)} %add.150), channel_id=1, source_target_pairs={{0,16},{16,0},{8,24},{24,8},{32,48},{48,32},{40,56},{56,40},{64,80... | collective-permute-start | bytes 44 | tf_op jit(solution)/shard_map/ppermute | solution.py:14
  202.5 4.2 %collective-permute-start.9 = (bf16[4,64,256]{2,1,0:T(8,128)(2,1)S(1)}, bf16[4,64,256]{2,1,0:T(8,128)(2,1)S(1)}, u32[]{:S(2)}, u32[]{:S(2)}) collective-permute-start(bf16[4,64,256]{2,1,0:T(8,128)(2,1)S(1)} %fusion.30), channel_id=1, source_target_pairs={{0,64},{64,0},{8,72},{72,8},{16,80},{80,16},{24,88},{88,24},{32,96... | collective-permute-start | bytes 393224 | tf_op jit(solution)/shard_map/ppermute | solution.py:14
  213.3 17.0 %psum.45 = f32[3]{0:T(128)S(1)} all-reduce(f32[3]{0:T(128)S(1)} %pad_maximum_fusion.3), channel_id=1, replica_groups=mesh['dp'=64,'tensor'=8] {'tensor'}, use_global_device_ids=true, to_apply=%region_15.16 | all-reduce | flops 3 | bytes 24 | tf_op jit(solution)/shard_map/psum | solution.py:46
  234.6 4.6 %collective-permute-start.11 = (f32[3]{0:T(128)S(1)}, f32[3]{0:T(128)S(1)}, u32[]{:S(2)}, u32[]{:S(2)}) collective-permute-start(f32[3]{0:T(128)S(1)} %add.156), channel_id=1, source_target_pairs={{0,16},{16,0},{8,24},{24,8},{32,48},{48,32},{40,56},{56,40},{64,80... | collective-permute-start | bytes 44 | tf_op jit(solution)/shard_map/ppermute | solution.py:14
  244.6 3.9 collective-permute-start.13
  253.0 7.4 %collective-permute-start.14 = (bf16[2,64,256]{2,1,0:T(8,128)(2,1)S(1)}, bf16[2,64,256]{2,1,0:T(8,128)(2,1)S(1)}, u32[]{:S(2)}, u32[]{:S(2)}) collective-permute-start(bf16[2,64,256]{2,1,0:T(8,128)(2,1)S(1)} %fusion.38), channel_id=1, source_target_pairs={{0,128},{128,0},{8,136},{136,8},{16,144},{144,16},{24,152},{152,24... | collective-permute-start | bytes 196616 | tf_op jit(solution)/shard_map/ppermute | solution.py:14
  264.8 18.8 %psum.46 = f32[3]{0:T(128)S(1)} all-reduce(f32[3]{0:T(128)S(1)} %pad_maximum_fusion.4), channel_id=1, replica_groups=mesh['dp'=64,'tensor'=8] {'tensor'}, use_global_device_ids=true, to_apply=%region_19.20 | all-reduce | flops 3 | bytes 24 | tf_op jit(solution)/shard_map/psum | solution.py:46
  287.8 4.6 %collective-permute-start.16 = (f32[3]{0:T(128)S(1)}, f32[3]{0:T(128)S(1)}, u32[]{:S(2)}, u32[]{:S(2)}) collective-permute-start(f32[3]{0:T(128)S(1)} %add.163), channel_id=1, source_target_pairs={{0,16},{16,0},{8,24},{24,8},{32,48},{48,32},{40,56},{56,40},{64,80... | collective-permute-start | bytes 44 | tf_op jit(solution)/shard_map/ppermute | solution.py:14
  297.8 4.1 %collective-permute-start.18 = (f32[3]{0:T(128)S(1)}, f32[3]{0:T(128)S(1)}, u32[]{:S(2)}, u32[]{:S(2)}) collective-permute-start(f32[3]{0:T(128)S(1)} %add.165), channel_id=1, source_target_pairs={{0,64},{64,0},{8,72},{72,8},{16,80},{80,16},{24,88},{88,24},{32,96... | collective-permute-start | bytes 44 | tf_op jit(solution)/shard_map/ppermute | solution.py:14
  303.0 7.8 %collective-permute-start.19 = (f32[3]{0:T(128)S(1)}, f32[3]{0:T(128)S(1)}, u32[]{:S(2)}, u32[]{:S(2)}) collective-permute-start(f32[3]{0:T(128)S(1)} %add.166), channel_id=1, source_target_pairs={{0,128},{128,0},{8,136},{136,8},{16,144},{144,16},{24,152},{152,24... | collective-permute-start | bytes 44 | tf_op jit(solution)/shard_map/ppermute | solution.py:14
  315.0 12.8 %collective-permute-start.20 = (bf16[1,64,256]{2,1,0:T(8,128)(2,1)S(1)}, bf16[1,64,256]{2,1,0:T(8,128)(2,1)S(1)}, u32[]{:S(2)}, u32[]{:S(2)}) collective-permute-start(bf16[1,64,256]{2,1,0:T(8,128)(2,1)S(1)} %select_bitcast_fusion.1), channel_id=1, source_target_pairs={{0,256},{256,0},{8,264},{264,8},{16,272},{272,16},{24,280},{280,24... | collective-permute-start | bytes 98312 | tf_op jit(solution)/shard_map/ppermute | solution.py:14
  331.8 19.0 %psum.47 = f32[3]{0:T(128)S(1)} all-reduce(f32[3]{0:T(128)S(1)} %pad_maximum_fusion.5), channel_id=1, replica_groups=mesh['dp'=64,'tensor'=8] {'tensor'}, use_global_device_ids=true, to_apply=%region_23.24 | all-reduce | flops 3 | bytes 24 | tf_op jit(solution)/shard_map/psum | solution.py:46
  355.1 4.6 %collective-permute-start.22 = (f32[3]{0:T(128)S(1)}, f32[3]{0:T(128)S(1)}, u32[]{:S(2)}, u32[]{:S(2)}) collective-permute-start(f32[3]{0:T(128)S(1)} %add.171), channel_id=1, source_target_pairs={{0,16},{16,0},{8,24},{24,8},{32,48},{48,32},{40,56},{56,40},{64,80... | collective-permute-start | bytes 44 | tf_op jit(solution)/shard_map/ppermute | solution.py:14
  370.3 7.0 %collective-permute-start.25 = (f32[3]{0:T(128)S(1)}, f32[3]{0:T(128)S(1)}, u32[]{:S(2)}, u32[]{:S(2)}) collective-permute-start(f32[3]{0:T(128)S(1)} %add.174), channel_id=1, source_target_pairs={{0,128},{128,0},{8,136},{136,8},{16,144},{144,16},{24,152},{152,24... | collective-permute-start | bytes 44 | tf_op jit(solution)/shard_map/ppermute | solution.py:14
  378.5 12.4 %collective-permute-start.26 = (f32[3]{0:T(128)S(1)}, f32[3]{0:T(128)S(1)}, u32[]{:S(2)}, u32[]{:S(2)}) collective-permute-start(f32[3]{0:T(128)S(1)} %add.175), channel_id=1, source_target_pairs={{0,256},{256,0},{8,264},{264,8},{16,272},{272,16},{24,280},{280,24... | collective-permute-start | bytes 44 | tf_op jit(solution)/shard_map/ppermute | solution.py:14
  (93 shorter events, 103.2 us)
Async XLA Ops:
  6.5 48.5 %all-gather.2.cloned.1.call-start = ((), (), s32[]{:S(2)}) async-start(), calls=%async_computation | async-start | bytes 4718592 | tf_op jit(solution)/shard_map/all_gather | solution.py:21
  58.7 26.5 %collective-permute-start = (bf16[32,64,256]{2,1,0:T(8,128)(2,1)S(1)}, bf16[32,64,256]{2,1,0:T(8,128)(2,1)}, u32[]{:S(2)}, u32[]{:S(2)}) collective-permute-start(bf16[32,64,256]{2,1,0:T(8,128)(2,1)S(1)} %select_bitcast_fusion), channel_id=1, source_target_pairs={{0,8},{8,0},{16,24},{24,16},{32,40},{40,32},{48,56},{56,48},{64,72... | collective-permute-start | bytes 3145736 | tf_op jit(solution)/shard_map/ppermute | solution.py:14
  103.7 4.3 %collective-permute-start.1 = (f32[3]{0:T(128)S(1)}, f32[3]{0:T(128)S(1)}, u32[]{:S(2)}, u32[]{:S(2)}) collective-permute-start(f32[3]{0:T(128)S(1)} %psum.42), channel_id=1, source_target_pairs={{0,8},{8,0},{16,24},{24,16},{32,40},{40,32},{48,56},{56,48},{64,72... | collective-permute-start | bytes 44 | tf_op jit(solution)/shard_map/ppermute | solution.py:14
  112.8 15.0 %collective-permute-start.2 = (bf16[16,64,256]{2,1,0:T(8,128)(2,1)S(1)}, bf16[16,64,256]{2,1,0:T(8,128)(2,1)S(1)}, u32[]{:S(2)}, u32[]{:S(2)}) collective-permute-start(bf16[16,64,256]{2,1,0:T(8,128)(2,1)S(1)} %fusion.16), channel_id=1, source_target_pairs={{0,16},{16,0},{8,24},{24,8},{32,48},{48,32},{40,56},{56,40},{64,80... | collective-permute-start | bytes 1572872 | tf_op jit(solution)/shard_map/ppermute | solution.py:14
  145.6 4.3 %collective-permute-start.3 = (f32[3]{0:T(128)S(1)}, f32[3]{0:T(128)S(1)}, u32[]{:S(2)}, u32[]{:S(2)}) collective-permute-start(f32[3]{0:T(128)S(1)} %psum.43), channel_id=1, source_target_pairs={{0,8},{8,0},{16,24},{24,16},{32,40},{40,32},{48,56},{56,48},{64,72... | collective-permute-start | bytes 44 | tf_op jit(solution)/shard_map/ppermute | solution.py:14
  149.8 5.8 %collective-permute-start.4 = (f32[3]{0:T(128)S(1)}, f32[3]{0:T(128)S(1)}, u32[]{:S(2)}, u32[]{:S(2)}) collective-permute-start(f32[3]{0:T(128)S(1)} %add.145), channel_id=1, source_target_pairs={{0,16},{16,0},{8,24},{24,8},{32,48},{48,32},{40,56},{56,40},{64,80... | collective-permute-start | bytes 44 | tf_op jit(solution)/shard_map/ppermute | solution.py:14
  159.0 7.1 %collective-permute-start.5 = (bf16[8,64,256]{2,1,0:T(8,128)(2,1)S(1)}, bf16[8,64,256]{2,1,0:T(8,128)(2,1)S(1)}, u32[]{:S(2)}, u32[]{:S(2)}) collective-permute-start(bf16[8,64,256]{2,1,0:T(8,128)(2,1)S(1)} %fusion.23), channel_id=1, source_target_pairs={{0,32},{32,0},{8,40},{40,8},{16,48},{48,16},{24,56},{56,24},{64,96... | collective-permute-start | bytes 786440 | tf_op jit(solution)/shard_map/ppermute | solution.py:14
  184.9 4.3 %collective-permute-start.6 = (f32[3]{0:T(128)S(1)}, f32[3]{0:T(128)S(1)}, u32[]{:S(2)}, u32[]{:S(2)}) collective-permute-start(f32[3]{0:T(128)S(1)} %psum.44), channel_id=1, source_target_pairs={{0,8},{8,0},{16,24},{24,16},{32,40},{40,32},{48,56},{56,48},{64,72... | collective-permute-start | bytes 44 | tf_op jit(solution)/shard_map/ppermute | solution.py:14
  189.2 5.8 %collective-permute-start.7 = (f32[3]{0:T(128)S(1)}, f32[3]{0:T(128)S(1)}, u32[]{:S(2)}, u32[]{:S(2)}) collective-permute-start(f32[3]{0:T(128)S(1)} %add.150), channel_id=1, source_target_pairs={{0,16},{16,0},{8,24},{24,8},{32,48},{48,32},{40,56},{56,40},{64,80... | collective-permute-start | bytes 44 | tf_op jit(solution)/shard_map/ppermute | solution.py:14
  194.9 4.3 %collective-permute-start.8 = (f32[3]{0:T(128)S(1)}, f32[3]{0:T(128)S(1)}, u32[]{:S(2)}, u32[]{:S(2)}) collective-permute-start(f32[3]{0:T(128)S(1)} %add.151), channel_id=1, source_target_pairs={{0,32},{32,0},{8,40},{40,8},{16,48},{48,16},{24,56},{56,24},{64,96... | collective-permute-start | bytes 44 | tf_op jit(solution)/shard_map/ppermute | solution.py:14
  202.5 8.0 %collective-permute-start.9 = (bf16[4,64,256]{2,1,0:T(8,128)(2,1)S(1)}, bf16[4,64,256]{2,1,0:T(8,128)(2,1)S(1)}, u32[]{:S(2)}, u32[]{:S(2)}) collective-permute-start(bf16[4,64,256]{2,1,0:T(8,128)(2,1)S(1)} %fusion.30), channel_id=1, source_target_pairs={{0,64},{64,0},{8,72},{72,8},{16,80},{80,16},{24,88},{88,24},{32,96... | collective-permute-start | bytes 393224 | tf_op jit(solution)/shard_map/ppermute | solution.py:14
  230.3 4.3 %collective-permute-start.10 = (f32[3]{0:T(128)S(1)}, f32[3]{0:T(128)S(1)}, u32[]{:S(2)}, u32[]{:S(2)}) collective-permute-start(f32[3]{0:T(128)S(1)} %psum.45), channel_id=1, source_target_pairs={{0,8},{8,0},{16,24},{24,16},{32,40},{40,32},{48,56},{56,48},{64,72... | collective-permute-start | bytes 44 | tf_op jit(solution)/shard_map/ppermute | solution.py:14
  234.6 5.8 %collective-permute-start.11 = (f32[3]{0:T(128)S(1)}, f32[3]{0:T(128)S(1)}, u32[]{:S(2)}, u32[]{:S(2)}) collective-permute-start(f32[3]{0:T(128)S(1)} %add.156), channel_id=1, source_target_pairs={{0,16},{16,0},{8,24},{24,8},{32,48},{48,32},{40,56},{56,40},{64,80... | collective-permute-start | bytes 44 | tf_op jit(solution)/shard_map/ppermute | solution.py:14
  240.4 4.3 %collective-permute-start.12 = (f32[3]{0:T(128)S(1)}, f32[3]{0:T(128)S(1)}, u32[]{:S(2)}, u32[]{:S(2)}) collective-permute-start(f32[3]{0:T(128)S(1)} %add.157), channel_id=1, source_target_pairs={{0,32},{32,0},{8,40},{40,8},{16,48},{48,16},{24,56},{56,24},{64,96... | collective-permute-start | bytes 44 | tf_op jit(solution)/shard_map/ppermute | solution.py:14
  244.6 5.2 %collective-permute-start.13 = (f32[3]{0:T(128)S(1)}, f32[3]{0:T(128)S(1)}, u32[]{:S(2)}, u32[]{:S(2)}) collective-permute-start(f32[3]{0:T(128)S(1)} %add.158), channel_id=1, source_target_pairs={{0,64},{64,0},{8,72},{72,8},{16,80},{80,16},{24,88},{88,24},{32,96... | collective-permute-start | bytes 44 | tf_op jit(solution)/shard_map/ppermute | solution.py:14
  253.0 9.0 %collective-permute-start.14 = (bf16[2,64,256]{2,1,0:T(8,128)(2,1)S(1)}, bf16[2,64,256]{2,1,0:T(8,128)(2,1)S(1)}, u32[]{:S(2)}, u32[]{:S(2)}) collective-permute-start(bf16[2,64,256]{2,1,0:T(8,128)(2,1)S(1)} %fusion.38), channel_id=1, source_target_pairs={{0,128},{128,0},{8,136},{136,8},{16,144},{144,16},{24,152},{152,24... | collective-permute-start | bytes 196616 | tf_op jit(solution)/shard_map/ppermute | solution.py:14
  287.8 5.8 %collective-permute-start.16 = (f32[3]{0:T(128)S(1)}, f32[3]{0:T(128)S(1)}, u32[]{:S(2)}, u32[]{:S(2)}) collective-permute-start(f32[3]{0:T(128)S(1)} %add.163), channel_id=1, source_target_pairs={{0,16},{16,0},{8,24},{24,8},{32,48},{48,32},{40,56},{56,40},{64,80... | collective-permute-start | bytes 44 | tf_op jit(solution)/shard_map/ppermute | solution.py:14
  297.8 5.2 %collective-permute-start.18 = (f32[3]{0:T(128)S(1)}, f32[3]{0:T(128)S(1)}, u32[]{:S(2)}, u32[]{:S(2)}) collective-permute-start(f32[3]{0:T(128)S(1)} %add.165), channel_id=1, source_target_pairs={{0,64},{64,0},{8,72},{72,8},{16,80},{80,16},{24,88},{88,24},{32,96... | collective-permute-start | bytes 44 | tf_op jit(solution)/shard_map/ppermute | solution.py:14
  303.0 8.8 %collective-permute-start.19 = (f32[3]{0:T(128)S(1)}, f32[3]{0:T(128)S(1)}, u32[]{:S(2)}, u32[]{:S(2)}) collective-permute-start(f32[3]{0:T(128)S(1)} %add.166), channel_id=1, source_target_pairs={{0,128},{128,0},{8,136},{136,8},{16,144},{144,16},{24,152},{152,24... | collective-permute-start | bytes 44 | tf_op jit(solution)/shard_map/ppermute | solution.py:14
  315.0 14.1 %collective-permute-start.20 = (bf16[1,64,256]{2,1,0:T(8,128)(2,1)S(1)}, bf16[1,64,256]{2,1,0:T(8,128)(2,1)S(1)}, u32[]{:S(2)}, u32[]{:S(2)}) collective-permute-start(bf16[1,64,256]{2,1,0:T(8,128)(2,1)S(1)} %select_bitcast_fusion.1), channel_id=1, source_target_pairs={{0,256},{256,0},{8,264},{264,8},{16,272},{272,16},{24,280},{280,24... | collective-permute-start | bytes 98312 | tf_op jit(solution)/shard_map/ppermute | solution.py:14
  355.1 5.8 %collective-permute-start.22 = (f32[3]{0:T(128)S(1)}, f32[3]{0:T(128)S(1)}, u32[]{:S(2)}, u32[]{:S(2)}) collective-permute-start(f32[3]{0:T(128)S(1)} %add.171), channel_id=1, source_target_pairs={{0,16},{16,0},{8,24},{24,8},{32,48},{48,32},{40,56},{56,40},{64,80... | collective-permute-start | bytes 44 | tf_op jit(solution)/shard_map/ppermute | solution.py:14
  365.2 5.2 %collective-permute-start.24 = (f32[3]{0:T(128)S(1)}, f32[3]{0:T(128)S(1)}, u32[]{:S(2)}, u32[]{:S(2)}) collective-permute-start(f32[3]{0:T(128)S(1)} %add.173), channel_id=1, source_target_pairs={{0,64},{64,0},{8,72},{72,8},{16,80},{80,16},{24,88},{88,24},{32,96... | collective-permute-start | bytes 44 | tf_op jit(solution)/shard_map/ppermute | solution.py:14
  370.3 8.2 %collective-permute-start.25 = (f32[3]{0:T(128)S(1)}, f32[3]{0:T(128)S(1)}, u32[]{:S(2)}, u32[]{:S(2)}) collective-permute-start(f32[3]{0:T(128)S(1)} %add.174), channel_id=1, source_target_pairs={{0,128},{128,0},{8,136},{136,8},{16,144},{144,16},{24,152},{152,24... | collective-permute-start | bytes 44 | tf_op jit(solution)/shard_map/ppermute | solution.py:14
  378.5 13.4 %collective-permute-start.26 = (f32[3]{0:T(128)S(1)}, f32[3]{0:T(128)S(1)}, u32[]{:S(2)}, u32[]{:S(2)}) collective-permute-start(f32[3]{0:T(128)S(1)} %add.175), channel_id=1, source_target_pairs={{0,256},{256,0},{8,264},{264,8},{16,272},{272,16},{24,280},{280,24... | collective-permute-start | bytes 44 | tf_op jit(solution)/shard_map/ppermute | solution.py:14
  (5 other events, 65.6 us)
Sparse Core Ops, SparseCore 0:
  9.5 45.5 all-gather.1
where the time goes:
time: 410 us; the launch traced here: 402 us
  starting transfers between devices  125 us (30%)
  waiting for transfers between devices  120 us (29%)
  blocking collectives  97.9 us (24%)
  between operations  28.6 us (7%)
  other arithmetic  23 us (6%)
    ppermute x27, starting transfers between devices, partner(): return lax.ppermute(block, axis, route)  125 us
    psum x6, blocking collectives, shards(): summed = lax.psum(partial_value, 'tensor')  97.9 us
    ppermute x27, waiting for transfers between devices, partner(): return lax.ppermute(block, axis, route)  71.7 us
    all_gather x1, waiting for transfers between devices, shards(): lax.all_gather(grad_out, 'tensor', axis=0, tiled=True)  47.8 us
    another operation x6, other arithmetic, shards(): jnp.stack([jnp.sum(first_f * second_f), jnp.sum(first_f * first_f), jnp.s...  11.8 us
    reduce_sum x6, other arithmetic, shards(): jnp.sum(first_f * second_f)  8.25 us
  transfers between devices with their start and end apart: 28, of which 28 were waited for; matrix products, arithmetic and copies ran while one was open for 0% of the time, Pallas kernels for 0%

commit v1 on v0

v1 whole, which is shorter than its diff:
```python
import functools

import jax
import jax.numpy as jnp
from jax import lax
from jax.experimental import pallas as pl
from jax.experimental.pallas import tpu as pltpu
from jax.sharding import PartitionSpec as P

MESH = pl.DeviceIdType.MESH
F32 = jnp.float32
BF16 = jnp.bfloat16

NX, NY, NZ = 4, 4, 16
NT = 2 * NY
EPS = 1e-6
ORDER = (0, 1, 3, 2)


def sum_rows(value):
    rows, lanes = value.shape
    part = value.reshape(rows // 8, 8, lanes).sum(axis=0)
    return sum(part[:, i : i + 128] for i in range(0, lanes, 128))


def coef(inner, own_sq):
    return 1.0 - inner / (2.0 * (jnp.maximum(own_sq, 0.0) + EPS))


def four_weights(p):
    c = [coef(p[i][i ^ 1], p[i][i]) for i in range(4)]

    def paired(i, j):
        return c[i] * (c[j] * p[i][j] + c[j + 1] * p[i][j + 1]) + c[i + 1] * (
            c[j] * p[i + 1][j] + c[j + 1] * p[i + 1][j + 1]
        )

    inner = paired(0, 2)
    low, high = coef(inner, paired(0, 0)), coef(inner, paired(2, 2))
    return [low * c[0], low * c[1], high * c[2], high * c[3]]


def tree_weights(gram):
    row = lax.broadcasted_iota(jnp.int32, gram.shape, 0)
    lane = lax.broadcasted_iota(jnp.int32, gram.shape, 1)
    col = lane & (NZ - 1)
    first = lane < NZ
    weight = None
    step = 1
    while step < NZ:
        diag, pair = col == row, col == (row ^ step)
        c_row = coef(
            jnp.sum(jnp.where(pair & first, gram, 0.0), axis=1, keepdims=True),
            jnp.sum(jnp.where(diag & first, gram, 0.0), axis=1, keepdims=True),
        )
        weight = c_row if weight is None else weight * c_row
        if 2 * step < NZ:
            c_col = coef(
                jnp.sum(jnp.where(pair, gram, 0.0), axis=0, keepdims=True),
                jnp.sum(jnp.where(diag, gram, 0.0), axis=0, keepdims=True),
            )
            gram = c_row * gram * c_col
            gram = gram + jnp.where(
                (row & step) != 0, pltpu.roll(gram, step, 0), pltpu.roll(gram, NZ - step, 0)
            )
            gram = gram + jnp.where(
                (col & step) != 0, pltpu.roll(gram, step, 1), pltpu.roll(gram, 128 - step, 1)
            )
        step *= 2
    return weight


def kernel(
    g_ref, a_ref, o_ref,
    gv, st, gb, ab, lbuf, cb, rb, yb, wv,
    gp1, g1t, g1x, g2t, g2x, g2z,
    in_sem, gs, gr, as_, ar, zs, zr,
    s1t, r1t, s1x, r1x, s2t, r2t, s2x, r2x, s2z, r2z,
):
    dp, t = lax.axis_index("dp"), lax.axis_index("tensor")
    z, x = dp // NX, dp % NX
    y, c = t // 2, t % 2
    tok = g_ref.shape[0]
    half = tok // 2
    block = o_ref.shape[0]

    def x_dev(i):
        return (z * NX + i, t)

    def t_dev(i):
        return (dp, i)

    def z_dev(i):
        return (i * NX + x, t)

    def send(src, dst, ssem, rsem, dev):
        copy = pltpu.make_async_remote_copy(
            src_ref=src, dst_ref=dst, send_sem=ssem, recv_sem=rsem,
            device_id=dev, device_id_type=MESH,
        )
        copy.start()
        return copy

    def arrived(dst, rsem):
        pltpu.make_async_copy(dst, dst, rsem).wait()

    load_g = pltpu.make_async_copy(g_ref, gv, in_sem.at[0])
    load_g.start()
    load_a = pltpu.make_async_copy(a_ref, ab.at[0], in_sem.at[1])
    load_a.start()

    barrier = pltpu.get_barrier_semaphore()
    for k in range(1, NX):
        pl.semaphore_signal(barrier, inc=1, device_id=x_dev((x + k) % NX), device_id_type=MESH)
    for k in range(1, NT):
        pl.semaphore_signal(barrier, inc=1, device_id=t_dev((t + k) % NT), device_id_type=MESH)

    def greet(k, _):
        pl.semaphore_signal(barrier, inc=1, device_id=z_dev((z + k) % NZ), device_id_type=MESH)
        return 0

    lax.fori_loop(1, NZ, greet, 0)

    load_g.wait()
    for i in range(NX):
        for k in range(NZ // 2):
            low, high = 64 * (2 * k * NX + i), 64 * ((2 * k + 1) * NX + i)
            st[i, :, 128 * k : 128 * k + 128] = jnp.concatenate(
                [gv[:, low : low + 64], gv[:, high : high + 64]], axis=1
            )
    mine = pl.ds(t * tok, tok)
    gb[0, mine, :] = st[x]
    load_a.wait()
    pl.semaphore_wait(barrier, NX + NT + NZ - 3)

    sent = []

    def rows(yy, cc, start=0, size=None):
        return pl.ds((yy * 2 + cc) * tok + start, tok if size is None else size)

    up, down, over = (y + 1) % NY, (y + NY - 1) % NY, (y + 2) % NY
    y_up, y_down, core = t_dev(up * 2 + c), t_dev(down * 2 + c), t_dev(y * 2 + 1 - c)

    def spread(d, region, k, dev):
        ref = gb.at[d, region]
        sent.append(send(ref, ref, gs.at[d, k], gr.at[d, k], dev))

    def landed(d, region, k):
        arrived(gb.at[d, region], gr.at[d, k])

    def start_block(d):
        if d:
            landed(d, mine, 0)
        spread(d, mine, 1, y_up)
        spread(d, mine, 2, y_down)
        spread(d, mine, 5, core)

    def forward_near(d):
        landed(d, rows(down, c), 1)
        spread(d, rows(down, c, 0, half), 3, y_up)
        landed(d, rows(up, c), 2)
        spread(d, rows(up, c, half, half), 4, y_down)
        spread(d, rows(down, c), 6, core)
        spread(d, rows(up, c), 7, core)

    def forward_far(d):
        landed(d, rows(over, c, 0, half), 3)
        spread(d, rows(over, c, 0, half), 8, core)
        landed(d, rows(over, c, half, half), 4)
        spread(d, rows(over, c, half, half), 9, core)

    def finish_block(d):
        landed(d, rows(y, 1 - c), 5)
        landed(d, rows(down, 1 - c), 6)
        landed(d, rows(up, 1 - c), 7)
        landed(d, rows(over, 1 - c, 0, half), 8)
        landed(d, rows(over, 1 - c, half, half), 9)

    tile = 256
    lanes = o_ref.shape[1]
    wide = gb.shape[2]

    def compute(d, before):
        r = (x + d) % NX
        others = before + [d]

        def body(i, accs):
            cols = pl.ds(pl.multiple_of(i * tile, tile), tile)
            value = lax.dot_general(
                gb[d, :, cols], ab[d], (((0,), (0,)), ((), ())), preferred_element_type=F32
            )
            lbuf[r, cols, :] = value
            out = []
            for acc, e in zip(accs, others):
                other = value if e == d else lbuf[(x + e) % NX, cols, :]
                out.append(acc + sum_rows(value * other))
            return tuple(out)

        zero = jnp.zeros((8, 128), F32)
        accs = lax.fori_loop(0, wide // tile, body, (zero,) * len(others))
        for acc, e in zip(accs, others):
            q = (x + e) % NX
            line = jnp.sum(acc, axis=0, keepdims=True)
            gp1[pl.ds(r * NX + q, 1), :] = line
            if e != d:
                gp1[pl.ds(q * NX + r, 1), :] = line

    for d in (1, 3, 2):
        sent.append(
            send(st.at[(x + d) % NX], gb.at[NX - d, mine], gs.at[d, 0], gr.at[NX - d, 0], x_dev((x + d) % NX))
        )
    start_block(0)
    right, left = x_dev((x + 1) % NX), x_dev((x + 3) % NX)
    sent.append(send(ab.at[0], ab.at[3], as_.at[0], ar.at[0], right))
    sent.append(send(ab.at[0], ab.at[1], as_.at[1], ar.at[1], left))
    start_block(1)
    start_block(3)
    forward_near(0)
    start_block(2)
    forward_near(1)
    forward_far(0)
    finish_block(0)
    compute(0, [])
    forward_near(3)
    forward_far(1)
    arows = ab.shape[1] // 2
    arrived(ab.at[3], ar.at[0])
    near = ab.at[3, pl.ds(0, arows)], ab.at[2, pl.ds(0, arows)]
    sent.append(send(*near, as_.at[2], ar.at[2], right))
    arrived(ab.at[1], ar.at[1])
    near = ab.at[1, pl.ds(arows, arows)], ab.at[2, pl.ds(arows, arows)]
    sent.append(send(*near, as_.at[3], ar.at[3], left))
    finish_block(1)
    compute(1, [0])
    forward_near(2)
    forward_far(3)
    finish_block(3)
    compute(3, [0, 1])
    forward_far(2)
    arrived(ab.at[2, pl.ds(0, arows)], ar.at[2])
    arrived(ab.at[2, pl.ds(arows, arows)], ar.at[3])
    finish_block(2)
    compute(2, [0, 1, 3])

    def total(buf, value, me, count, dev_of, ssem, rsem):
        buf[me] = value

        def out(k, _):
            send(buf.at[me], buf.at[me], ssem.at[k], rsem.at[me], dev_of((me + k) % count))
            return 0

        def back(k, _):
            q = (me + k) % count
            arrived(buf.at[q], rsem.at[q])
            return 0

        def done(k, _):
            pltpu.make_async_copy(buf.at[me], buf.at[me], ssem.at[k]).wait()
            return 0

        lax.fori_loop(1, count, out, 0)
        lax.fori_loop(1, count, back, 0)
        lax.fori_loop(1, count, done, 0)
        return sum(buf[i] for i in range(count))

    part = total(g1t, gp1[...], t, NT, t_dev, s1t, r1t)
    part = total(g1x, part, x, NX, x_dev, s1x, r1x)
    part = jnp.broadcast_to(jnp.sum(part, axis=1, keepdims=True), part.shape)
    inner = [[part[i * NX + j : i * NX + j + 1] for j in range(NX)] for i in range(NX)]
    w4 = [jnp.concatenate([w] * (lanes // 128), axis=1) for w in four_weights(inner)]

    def combined(b):
        region = pl.ds(pl.multiple_of(b * block, block), block)
        return sum(w4[i] * lbuf[i, region, :] for i in range(NX)).astype(BF16)

    def z_out(k, _):
        b = (z + k) % NZ
        cb[b] = combined(b)
        send(cb.at[b], rb.at[z], zs.at[k], zr.at[z], z_dev(b))
        return 0

    for k in (8, 7, 9, 6, 10, 5, 11, 4, 12, 3, 13, 2, 14, 1, 15):
        z_out(k, 0)
    rb[z] = combined(z)


    for k in (0, 1, 15, 2, 14, 3, 13, 4, 12, 5, 11, 6, 10, 7, 9, 8):
        if k:
            q = (z + k) % NZ
            arrived(rb.at[q], zr.at[q])
        q = (z + k) % NZ
        for i in range(lanes // 128):
            yb[i, pl.ds(q, block, stride=NZ), :] = rb[q, :, 128 * i : 128 * i + 128].astype(F32)

    def square(i, acc):
        for j in range(lanes // 128):
            part = yb[j, pl.ds(pl.multiple_of(i * 128, 128), 128), :].astype(BF16)
            acc = acc + lax.dot_general(
                part, part, (((1,), (1,)), ((), ())), preferred_element_type=F32
            )
        return acc

    gram = lax.fori_loop(0, block * NZ // 128, square, jnp.zeros((128, 128), F32))
    same = (lax.broadcasted_iota(jnp.int32, (128, 128), 0) // NZ) == (
        lax.broadcasted_iota(jnp.int32, (128, 128), 1) // NZ
    )
    gram = jnp.where(same, gram, 0.0).reshape(128 // NZ, NZ, 128).sum(axis=0)
    gram = total(g2t, gram, t, NT, t_dev, s2t, r2t)
    gram = total(g2x, gram, x, NX, x_dev, s2x, r2x)
    gram = total(g2z, gram, z, NZ, z_dev, s2z, r2z)
    for shift in (NZ, 2 * NZ, 4 * NZ):
        gram = gram + pltpu.roll(gram, shift, 1)
    wv[...] = jnp.broadcast_to(tree_weights(gram), (NZ, lanes))
    o_ref[...] = sum(wv[i : i + 1, :] * rb[i].astype(F32) for i in range(NZ)).astype(BF16)

    for copy in sent:
        copy.wait_send()

    def z_done(k, _):
        pltpu.make_async_copy(cb.at[0], cb.at[0], zs.at[k]).wait()
        return 0

    lax.fori_loop(1, NZ, z_done, 0)


def shards(grad_out, attn_out):
    tok, width = grad_out.shape
    rows, lanes = attn_out.shape
    wide, block = width // NX, width // (NX * NZ)
    dma, reg = pltpu.SemaphoreType.DMA, pltpu.VMEM
    return pl.pallas_call(
        kernel,
        out_shape=jax.ShapeDtypeStruct((block, lanes), BF16),
        in_specs=[pl.BlockSpec(memory_space=pl.ANY)] * 2,
        out_specs=pl.BlockSpec(memory_space=pltpu.VMEM),
        scratch_shapes=[
            reg((tok, width), BF16),
            reg((NX, tok, wide), BF16),
            reg((NX, rows, wide), BF16),
            reg((NX, rows, lanes), BF16),
            reg((NX, wide, lanes), F32),
            reg((NZ, block, lanes), BF16),
            reg((NZ, block, lanes), BF16),
            reg((lanes // 128, NZ * block, 128), F32),
            reg((NZ, lanes), F32),
            reg((NX * NX, 128), F32),
            reg((NT, NX * NX, 128), F32),
            reg((NX, NX * NX, 128), F32),
            reg((NT, NZ, 128), F32),
            reg((NX, NZ, 128), F32),
            reg((NZ, NZ, 128), F32),
            dma((2,)),
            dma((NX, 10)), dma((NX, 10)),
            dma((4,)), dma((4,)),
            dma((NZ,)), dma((NZ,)),
            dma((NT,)), dma((NT,)),
            dma((NX,)), dma((NX,)),
            dma((NT,)), dma((NT,)),
            dma((NX,)), dma((NX,)),
            dma((NZ,)), dma((NZ,)),
        ],
        compiler_params=pltpu.CompilerParams(
            collective_id=0, has_side_effects=True, vmem_limit_bytes=40 * 1024 * 1024
        ),
        name="adasum",
    )(grad_out, attn_out)


def solution(mesh):
    return jax.shard_map(
        shards,
        mesh=mesh,
        in_specs=(P(("dp", "tensor"), None), P("dp", "tensor")),
        out_specs=P("dp", "tensor"),
        check_vma=False,
    )
```

time: 410 us -> 97.7 us (0.24); the launches traced: 402 us -> 96.9 us
  starting transfers between devices: 125 us -> 0 us
  waiting for transfers between devices: 120 us -> 0 us
  blocking collectives: 97.9 us -> 0 us
  Pallas kernels: 0 us -> 94.3 us
  between operations: 28.6 us -> 0.01 us
  other arithmetic: 23 us -> 0 us
    ppermute x27 -> x0, starting transfers between devices: 125 us -> none  [partner(): return lax.ppermute(block, axis, route)]
    psum x6 -> x0, blocking collectives: 97.9 us -> none  [shards(): summed = lax.psum(partial_value, 'tensor')]
    pallas_call x0 -> x1, Pallas kernels: none -> 94.3 us  [shards(): pl.pallas_call(kernel, out_shape=jax.ShapeDtypeStruct((block, lanes), BF1...]
    ppermute x27 -> x0, waiting for transfers between devices: 71.7 us -> none  [partner(): return lax.ppermute(block, axis, route)]
    all_gather x1 -> x0, waiting for transfers between devices: 47.8 us -> none  [shards(): lax.all_gather(grad_out, 'tensor', axis=0, tiled=True)]
    another operation x6 -> x0, other arithmetic: 11.8 us -> none  [shards(): jnp.stack([jnp.sum(first_f * second_f), jnp.sum(first_f * first_f), jnp.s...]
    reduce_sum x6 -> x0, other arithmetic: 8.25 us -> none  [shards(): jnp.sum(first_f * second_f)]
  transfers between devices with their start and end apart: 28 -> 0, of which waited for: 28 -> 0; matrix products, arithmetic and copies ran while one was open for 0% -> 0% of each run, Pallas kernels for 0% -> 0%
where the time goes in v1:
time: 97.7 us; the launch traced here: 96.9 us
  Pallas kernels  94.3 us (97%)
  local copies, waits for them, and re-layouts  2.61 us (3%)
    pallas_call x1, Pallas kernels, shards(): pl.pallas_call(kernel, out_shape=jax.ShapeDtypeStruct((block, lanes), BF1...  94.3 us
    unnamed x5, local copies, waits for them, and re-layouts  2.61 us

profile of v1, /device:TPU:1, one launch (start us, length us, event | category | flops | bytes accessed | tf_op | source)
XLA Modules:
  0.0 96.9 jit_solution(9032618575966668469)
XLA Ops:
  0.0 0.0 copy-start
  0.0 1.0 %copy-done = bf16[64,4096]{1,0:T(8,128)(2,1)S(1)} copy-done((bf16[64,4096]{1,0:T(8,128)(2,1)S(1)}, bf16[64,4096]{1,0:T(8,128)(2,1)}, u32[]{:S(2)}) %copy-start) | copy-done | bytes 524312
  1.0 0.0 copy-start.1
  1.0 0.9 copy-done.1
  2.0 94.3 %adasum.1 = bf16[64,256]{1,0:T(8,128)(2,1)S(1)} custom-call(bf16[64,4096]{1,0:T(8,128)(2,1)S(1)} %copy-done, bf16[512,256]{1,0:T(8,128)(2,1)S(1)} %copy-done.1), custom_call_target="tpu_custom_call" | custom-call | tf_op jit(solution)/shard_map/adasum/pallas_call | solution.py:331
  96.3 0.6 copy.4
Async XLA Ops:
  0.0 1.0 %copy-start = (bf16[64,4096]{1,0:T(8,128)(2,1)S(1)}, bf16[64,4096]{1,0:T(8,128)(2,1)}, u32[]{:S(2)}) copy-start(bf16[64,4096]{1,0:T(8,128)(2,1)} %g_ref.1) | copy-start | bytes 1572868
  1.0 0.9 copy-start.1

commit v2 on v0

v2 whole, which is shorter than its diff:
```python
import jax
import jax.numpy as jnp
from jax import lax
from jax.experimental import pallas as pl
from jax.experimental.pallas import tpu as pltpu
from jax.sharding import PartitionSpec as P

MESH = pl.DeviceIdType.MESH
F32 = jnp.float32
BF16 = jnp.bfloat16

NX, NY, NZ = 4, 4, 16
NT = 2 * NY
NP = NZ // 2
GROUP = 2 * NX
EPS = 1e-6
ORDER = (0, 1, 3, 4, 2, 5, 7, 6)


def sum_rows(value):
    rows, lanes = value.shape
    part = value.reshape(rows // 8, 8, lanes).sum(axis=0)
    return sum(part[:, i : i + 128] for i in range(0, lanes, 128))


def coef(inner, own_sq):
    return 1.0 - inner / (2.0 * (jnp.maximum(own_sq, 0.0) + EPS))


def pack(lines):
    each = jnp.sum(lines, axis=1, keepdims=True)
    row = lax.broadcasted_iota(jnp.int32, lines.shape, 0)
    lane = lax.broadcasted_iota(jnp.int32, lines.shape, 1)
    return jnp.sum(jnp.where(row == lane, each, 0.0), axis=0, keepdims=True)


def tree_weights(line):
    n = 8
    row = lax.broadcasted_iota(jnp.int32, (n, 128), 0)
    lane = lax.broadcasted_iota(jnp.int32, (n, 128), 1)
    col = lane & (n - 1)
    gram = jnp.where(lane // n == row, jnp.broadcast_to(line, (n, 128)), 0.0)
    for shift in (8, 16, 32, 64):
        gram = gram + pltpu.roll(gram, shift, 1)
    first = lane < n
    weight = None
    step = 1
    while step < n:
        diag, pair = col == row, col == (row ^ step)
        c_row = coef(
            jnp.sum(jnp.where(pair & first, gram, 0.0), axis=1, keepdims=True),
            jnp.sum(jnp.where(diag & first, gram, 0.0), axis=1, keepdims=True),
        )
        weight = c_row if weight is None else weight * c_row
        if 2 * step < n:
            c_col = coef(
                jnp.sum(jnp.where(pair, gram, 0.0), axis=0, keepdims=True),
                jnp.sum(jnp.where(diag, gram, 0.0), axis=0, keepdims=True),
            )
            gram = c_row * gram * c_col
            gram = gram + jnp.where(
                (row & step) != 0, pltpu.roll(gram, step, 0), pltpu.roll(gram, n - step, 0)
            )
            gram = gram + jnp.where(
                (col & step) != 0, pltpu.roll(gram, step, 1), pltpu.roll(gram, 128 - step, 1)
            )
        step *= 2
    return weight


def kernel(
    g_ref, a_ref, o_ref,
    gv, st, gb, ab, lbuf, cb, rb, rf, wv, gp1, gp2,
    line1, slots1, line2, slots2, line3, slots3,
    in_sem, gs, gr, as_, ar, zs, zr, sums,
):
    dp, t = lax.axis_index("dp"), lax.axis_index("tensor")
    z, x = dp // NX, dp % NX
    zp, zb = z // 2, z % 2
    y, c = t // 2, t % 2
    tok = g_ref.shape[0]
    half = tok // 2
    block, lanes = o_ref.shape
    wide = gb.shape[2]

    def dev(xx, zz, tt):
        return (zz * NX + xx, tt)

    def group_dev(i):
        return dev(i // NT % NX, zp * 2 + i // (NT * NX), i % NT)

    def plane_dev(i):
        return dev(i // NT, z, i % NT)

    def z_dev(i):
        return dev(x, i, t)

    me_group, me_plane = (zb * NX + x) * NT + t, x * NT + t

    def send(src, dst, ssem, rsem, to):
        copy = pltpu.make_async_remote_copy(
            src_ref=src, dst_ref=dst, send_sem=ssem, recv_sem=rsem,
            device_id=to, device_id_type=MESH,
        )
        copy.start()
        return copy

    def arrived(dst, rsem):
        pltpu.make_async_copy(dst, dst, rsem).wait()

    load_g = pltpu.make_async_copy(g_ref, gv, in_sem.at[0])
    load_g.start()
    load_a = pltpu.make_async_copy(a_ref, ab.at[0], in_sem.at[1])
    load_a.start()

    barrier = pltpu.get_barrier_semaphore()

    def greet(dev_of, me, count):
        def body(k, _):
            to = dev_of((me + k) % count)
            pl.semaphore_signal(barrier, inc=1, device_id=to, device_id_type=MESH)
            return 0

        lax.fori_loop(1, count, body, 0)

    greet(group_dev, me_group, GROUP * NT)
    greet(z_dev, z, NZ)

    load_g.wait()
    for i in range(NX):
        for k in range(NZ // 2):
            par, pos = k // (NP // 2), 2 * (k % (NP // 2))
            low, high = (64 * (NX * (2 * p + par) + i) for p in (pos, pos + 1))
            st[par * NX + i, :, 64 * pos : 64 * pos + 128] = jnp.concatenate(
                [gv[:, low : low + 64], gv[:, high : high + 64]], axis=1
            )
    mine = pl.ds(t * tok, tok)
    gb[0, mine, :] = st[zb * NX + x]
    load_a.wait()
    pl.semaphore_wait(barrier, GROUP * NT - 1 + NZ - 1)

    sent = []

    def rows(yy, cc, start=0, size=None):
        return pl.ds((yy * 2 + cc) * tok + start, tok if size is None else size)

    def beside(e):
        return (x + e % NX) % NX, zp * 2 + (zb + e // NX) % 2

    up, down, over = (y + 1) % NY, (y + NY - 1) % NY, (y + 2) % NY
    y_up, y_down, core = (dev(x, z, i) for i in (up * 2 + c, down * 2 + c, y * 2 + 1 - c))

    def give(e):
        xx, zz = beside(e)
        back = e // NX * NX + (NX - e % NX) % NX
        src = st.at[zz % 2 * NX + xx]
        sent.append(send(src, gb.at[back, mine], gs.at[e, 0], gr.at[back, 0], dev(xx, zz, t)))

    def spread(e, region, k, to):
        ref = gb.at[e, region]
        sent.append(send(ref, ref, gs.at[e, k], gr.at[e, k], to))

    def landed(e, region, k):
        arrived(gb.at[e, region], gr.at[e, k])

    def start(e):
        if e:
            landed(e, mine, 0)
        spread(e, mine, 1, y_up)
        spread(e, mine, 2, y_down)
        spread(e, mine, 5, core)

    def near(e):
        landed(e, rows(down, c), 1)
        spread(e, rows(down, c, 0, half), 3, y_up)
        landed(e, rows(up, c), 2)
        spread(e, rows(up, c, half, half), 4, y_down)
        spread(e, rows(down, c), 6, core)
        spread(e, rows(up, c), 7, core)

    def far(e):
        landed(e, rows(over, c, 0, half), 3)
        landed(e, rows(over, c, half, half), 4)
        spread(e, rows(over, c), 8, core)

    def whole(e):
        landed(e, rows(y, 1 - c), 5)
        landed(e, rows(down, 1 - c), 6)
        landed(e, rows(up, 1 - c), 7)
        landed(e, rows(over, 1 - c), 8)

    arows = ab.shape[1] // 2
    low, high, full = pl.ds(0, arows), pl.ds(arows, arows), pl.ds(0, 2 * arows)
    right, left = dev((x + 1) % NX, z, t), dev((x + 3) % NX, z, t)
    across = dev(x, zp * 2 + 1 - zb, t)

    def pass_on(e, to_e, part, k, to):
        sent.append(send(ab.at[e, part], ab.at[to_e, part], as_.at[k], ar.at[k], to))

    def have(e, part, k):
        arrived(ab.at[e, part], ar.at[k])

    def heads_start():
        pass_on(0, 3, full, 0, right)
        pass_on(0, 1, full, 1, left)
        pass_on(0, 4, full, 2, across)

    def heads_near():
        have(3, full, 0)
        pass_on(3, 2, low, 3, right)
        pass_on(3, 7, high, 5, across)
        have(1, full, 1)
        pass_on(1, 2, high, 4, left)
        pass_on(1, 5, low, 6, across)

    def heads_across():
        have(4, full, 2)
        pass_on(4, 7, low, 7, right)
        pass_on(4, 5, high, 8, left)

    def heads_far():
        have(7, low, 7)
        pass_on(7, 6, low, 9, right)
        have(5, high, 8)
        pass_on(5, 6, high, 10, left)

    heads_needs = {
        2: ((low, 3), (high, 4)),
        5: ((low, 6),),
        7: ((high, 5),),
        6: ((low, 9), (high, 10)),
    }
    tile = 256

    def index(e):
        return (zb + e // NX) % 2 * NX + (x + e % NX) % NX

    def put(gp, i, j, acc):
        line = jnp.sum(acc, axis=0, keepdims=True)
        gp[pl.ds(i * 8 + j, 1), :] = line
        gp[pl.ds(j * 8 + i, 1), :] = line

    def compute(e, before):
        for part, k in heads_needs.get(e, ()):
            have(e, part, k)
        r = index(e)
        others = before + [e]

        def body(i, accs):
            cols = pl.ds(pl.multiple_of(i * tile, tile), tile)
            value = lax.dot_general(
                gb[e, :, cols], ab[e], (((0,), (0,)), ((), ())), preferred_element_type=F32
            )
            lbuf[r, cols, :] = value
            out = []
            for acc, o in zip(accs, others):
                other = value if o == e else lbuf[index(o), cols, :]
                out.append(acc + sum_rows(value * other))
            return tuple(out)

        zero = jnp.zeros((8, 128), F32)
        accs = lax.fori_loop(0, wide // tile, body, (zero,) * len(others))
        for acc, o in zip(accs, others):
            put(gp1, r, index(o), acc)

    for e in ORDER[1:]:
        give(e)
    start(0)
    done = []

    def finish(e):
        whole(e)
        compute(e, list(done))
        done.append(e)

    start(1)
    start(3)
    start(4)
    heads_start()
    near(0)
    start(2)
    start(5)
    start(7)
    near(1)
    far(0)
    start(6)
    near(3)
    far(1)
    finish(0)
    near(4)
    far(3)
    heads_across()
    heads_near()
    finish(1)
    near(2)
    far(4)
    finish(3)
    near(5)
    far(2)
    finish(4)
    near(7)
    far(5)
    heads_far()
    near(6)
    finish(2)
    far(7)
    finish(5)
    far(6)
    finish(7)
    finish(6)

    def total(line, slots, value, me, count, dev_of, k):
        line[...] = value
        keep = pltpu.make_async_copy(line, slots.at[pl.ds(me, 1)], sums.at[k, 1])
        keep.start()

        def out(i, _):
            send(line, slots.at[pl.ds(me, 1)], sums.at[k, 0], sums.at[k, 1], dev_of((me + i) % count))
            return 0

        lax.fori_loop(1, count, out, 0)
        every = slots.at[pl.ds(0, count)]
        pltpu.make_async_copy(every, every, sums.at[k, 1]).wait()
        others = slots.at[pl.ds(0, count - 1)]
        pltpu.make_async_copy(others, others, sums.at[k, 0]).wait()
        return jnp.sum(slots[...], axis=0, keepdims=True)

    line = total(line1, slots1, pack(gp1[...]), me_group, GROUP * NT, group_dev, 0)
    wv[...] = jnp.broadcast_to(tree_weights(line), wv.shape)
    w8 = [wv[i : i + 1, :] for i in range(GROUP)]

    def combined(b):
        region = pl.ds(pl.multiple_of(b * block, block), block)
        return sum(w8[i] * lbuf[i, region, :] for i in range(GROUP)).astype(BF16)

    for k in (4, 3, 5, 2, 6, 1, 7):
        b = (zp + k) % NP
        cb[b] = combined(b)
        sent.append(send(cb.at[b], rb.at[zp], zs.at[k], zr.at[zp], z_dev(2 * b + zb)))
    rb[zp] = combined(zp)

    places = []
    for k in (0, 1, 7, 2, 6, 3, 5, 4):
        q = (zp + k) % NP
        if k:
            arrived(rb.at[q], zr.at[q])
        value = rb[q].astype(F32)
        rf[q] = value
        for o in places:
            put(gp2, q, o, sum_rows(value * rf[o]))
        put(gp2, q, q, sum_rows(value * value))
        places.append(q)

    line = total(line2, slots2, pack(gp2[...]), me_plane, NX * NT, plane_dev, 1)
    line = total(line3, slots3, line, z, NZ, z_dev, 2)
    wv[...] = jnp.broadcast_to(tree_weights(line), wv.shape)
    o_ref[...] = sum(wv[i : i + 1, :] * rf[i] for i in range(NP)).astype(BF16)

    for copy in sent:
        copy.wait_send()


def shards(grad_out, attn_out):
    tok, width = grad_out.shape
    rows, lanes = attn_out.shape
    wide, block = width // GROUP, width // (NX * NZ)
    dma, reg = pltpu.SemaphoreType.DMA, pltpu.VMEM
    return pl.pallas_call(
        kernel,
        out_shape=jax.ShapeDtypeStruct((block, lanes), BF16),
        in_specs=[pl.BlockSpec(memory_space=pl.ANY)] * 2,
        out_specs=pl.BlockSpec(memory_space=pltpu.VMEM),
        scratch_shapes=[
            reg((tok, width), BF16),
            reg((GROUP, tok, wide), BF16),
            reg((GROUP, rows, wide), BF16),
            reg((GROUP, rows, lanes), BF16),
            reg((GROUP, wide, lanes), F32),
            reg((NP, block, lanes), BF16),
            reg((NP, block, lanes), BF16),
            reg((NP, block, lanes), F32),
            reg((8, lanes), F32),
            reg((64, 128), F32),
            reg((64, 128), F32),
            reg((1, 128), F32), reg((GROUP * NT, 128), F32),
            reg((1, 128), F32), reg((NX * NT, 128), F32),
            reg((1, 128), F32), reg((NZ, 128), F32),
            dma((2,)),
            dma((GROUP, 9)), dma((GROUP, 9)),
            dma((11,)), dma((11,)),
            dma((NP,)), dma((NP,)),
            dma((3, 2)),
        ],
        compiler_params=pltpu.CompilerParams(
            collective_id=0, has_side_effects=True, vmem_limit_bytes=60 * 1024 * 1024
        ),
        name="adasum",
    )(grad_out, attn_out)


def solution(mesh):
    return jax.shard_map(
        shards,
        mesh=mesh,
        in_specs=(P(("dp", "tensor"), None), P("dp", "tensor")),
        out_specs=P("dp", "tensor"),
        check_vma=False,
    )
```

time: 410 us -> 85.7 us (0.21); the launches traced: 402 us -> 85.5 us
  starting transfers between devices: 125 us -> 0 us
  waiting for transfers between devices: 120 us -> 0 us
  blocking collectives: 97.9 us -> 0 us
  Pallas kernels: 0 us -> 84.1 us
  between operations: 28.6 us -> 0.01 us
  other arithmetic: 23 us -> 0 us
    ppermute x27 -> x0, starting transfers between devices: 125 us -> none  [partner(): return lax.ppermute(block, axis, route)]
    psum x6 -> x0, blocking collectives: 97.9 us -> none  [shards(): summed = lax.psum(partial_value, 'tensor')]
    pallas_call x0 -> x1, Pallas kernels: none -> 84.1 us  [shards(): pl.pallas_call(kernel, out_shape=jax.ShapeDtypeStruct((block, lanes), BF1...]
    ppermute x27 -> x0, waiting for transfers between devices: 71.7 us -> none  [partner(): return lax.ppermute(block, axis, route)]
    all_gather x1 -> x0, waiting for transfers between devices: 47.8 us -> none  [shards(): lax.all_gather(grad_out, 'tensor', axis=0, tiled=True)]
    another operation x6 -> x0, other arithmetic: 11.8 us -> none  [shards(): jnp.stack([jnp.sum(first_f * second_f), jnp.sum(first_f * first_f), jnp.s...]
    reduce_sum x6 -> x0, other arithmetic: 8.25 us -> none  [shards(): jnp.sum(first_f * second_f)]
  transfers between devices with their start and end apart: 28 -> 0, of which waited for: 28 -> 0; matrix products, arithmetic and copies ran while one was open for 0% -> 0% of each run, Pallas kernels for 0% -> 0%
where the time goes in v2:
time: 85.7 us; the launch traced here: 85.5 us
  Pallas kernels  84.1 us (98%)
  local copies, waits for them, and re-layouts  1.38 us (2%)
    pallas_call x1, Pallas kernels, shards(): pl.pallas_call(kernel, out_shape=jax.ShapeDtypeStruct((block, lanes), BF1...  84.1 us

profile of v2, /device:TPU:1, one launch (start us, length us, event | category | flops | bytes accessed | tf_op | source)
XLA Modules:
  0.0 85.5 jit_solution(18291720953702970365)
XLA Ops:
  0.0 84.1 %adasum.1 = bf16[64,256]{1,0:T(8,128)(2,1)} custom-call(bf16[64,4096]{1,0:T(8,128)(2,1)} %g_ref.1, bf16[512,256]{1,0:T(8,128)(2,1)} %a_ref.1), custom_call_target="tpu_custom_call" | custom-call | tf_op jit(solution)/shard_map/adasum/pallas_call | solution.py:368
  84.1 1.4 %copy.4 = bf16[64,256]{1,0:T(8,128)(2,1)} copy(bf16[64,256]{1,0:T(8,128)(2,1)} %adasum.1) | data formatting | bytes 65536

commit v3 on v2

--- a/solution.py
+++ b/solution.py
@@ -14,7 +14,10 @@
 NP = NZ // 2
 GROUP = 2 * NX
 EPS = 1e-6
-ORDER = (0, 1, 3, 4, 2, 5, 7, 6)
+ORDER = (0, 1, 3, 4, 5, 7, 2, 6)
+AHEAD = 4
+DIRECT = (0, 6)
+HEADS = (3, 5)
 
 
 def sum_rows(value):
@@ -72,7 +75,7 @@
     g_ref, a_ref, o_ref,
     gv, st, gb, ab, lbuf, cb, rb, rf, wv, gp1, gp2,
     line1, slots1, line2, slots2, line3, slots3,
-    in_sem, gs, gr, as_, ar, zs, zr, sums,
+    in_sem, gs, gr, as_, ar, zs, zr, sums, heard,
 ):
     dp, t = lax.axis_index("dp"), lax.axis_index("tensor")
     z, x = dp // NX, dp % NX
@@ -115,16 +118,21 @@
 
     barrier = pltpu.get_barrier_semaphore()
 
-    def greet(dev_of, me, count):
-        def body(k, _):
-            to = dev_of((me + k) % count)
-            pl.semaphore_signal(barrier, inc=1, device_id=to, device_id_type=MESH)
-            return 0
-
-        lax.fori_loop(1, count, body, 0)
-
-    greet(group_dev, me_group, GROUP * NT)
-    greet(z_dev, z, NZ)
+    up, down, over = (y + 1) % NY, (y + NY - 1) % NY, (y + 2) % NY
+    y_up, y_down, core = (dev(x, z, i) for i in (up * 2 + c, down * 2 + c, y * 2 + 1 - c))
+    z_up, z_down = z_dev((z + 2) % NZ), z_dev((z + NZ - 2) % NZ)
+
+    def beside(e):
+        return (x + e % NX) % NX, zp * 2 + (zb + e // NX) % 2
+
+    def greet(k, _):
+        to = group_dev((me_group + k) % (GROUP * NT))
+        pl.semaphore_signal(barrier, inc=1, device_id=to, device_id_type=MESH)
+        return 0
+
+    lax.fori_loop(1, GROUP * NT, greet, 0)
+    for to in (z_up, z_down):
+        pl.semaphore_signal(barrier, inc=1, device_id=to, device_id_type=MESH)
 
     load_g.wait()
     for i in range(NX):
@@ -137,18 +145,12 @@
     mine = pl.ds(t * tok, tok)
     gb[0, mine, :] = st[zb * NX + x]
     load_a.wait()
-    pl.semaphore_wait(barrier, GROUP * NT - 1 + NZ - 1)
+    pl.semaphore_wait(barrier, GROUP * NT + 1)
 
     sent = []
 
     def rows(yy, cc, start=0, size=None):
         return pl.ds((yy * 2 + cc) * tok + start, tok if size is None else size)
-
-    def beside(e):
-        return (x + e % NX) % NX, zp * 2 + (zb + e // NX) % 2
-
-    up, down, over = (y + 1) % NY, (y + NY - 1) % NY, (y + 2) % NY
-    y_up, y_down, core = (dev(x, z, i) for i in (up * 2 + c, down * 2 + c, y * 2 + 1 - c))
 
     def give(e):
         xx, zz = beside(e)
@@ -168,19 +170,26 @@
             landed(e, mine, 0)
         spread(e, mine, 1, y_up)
         spread(e, mine, 2, y_down)
+        if e in DIRECT:
+            spread(e, mine, 3, dev(x, z, over * 2 + c))
         spread(e, mine, 5, core)
 
     def near(e):
         landed(e, rows(down, c), 1)
-        spread(e, rows(down, c, 0, half), 3, y_up)
+        if e not in DIRECT:
+            spread(e, rows(down, c, 0, half), 3, y_up)
         landed(e, rows(up, c), 2)
-        spread(e, rows(up, c, half, half), 4, y_down)
+        if e not in DIRECT:
+            spread(e, rows(up, c, half, half), 4, y_down)
         spread(e, rows(down, c), 6, core)
         spread(e, rows(up, c), 7, core)
 
     def far(e):
-        landed(e, rows(over, c, 0, half), 3)
-        landed(e, rows(over, c, half, half), 4)
+        if e in DIRECT:
+            landed(e, rows(over, c), 3)
+        else:
+            landed(e, rows(over, c, 0, half), 3)
+            landed(e, rows(over, c, half, half), 4)
         spread(e, rows(over, c), 8, core)
 
     def whole(e):
@@ -263,9 +272,6 @@
         for acc, o in zip(accs, others):
             put(gp1, r, index(o), acc)
 
-    for e in ORDER[1:]:
-        give(e)
-    start(0)
     done = []
 
     def finish(e):
@@ -273,41 +279,42 @@
         compute(e, list(done))
         done.append(e)
 
-    start(1)
-    start(3)
-    start(4)
+    def hear(step):
+        if step > 1:
+            pl.semaphore_wait(heard.at[step - 2, 0], 1)
+            pl.semaphore_wait(heard.at[step - 2, 1], 1)
+        if step < NP // 2:
+            for side, to in enumerate((z_up, z_down)):
+                pl.semaphore_signal(heard.at[step - 1, side], inc=1, device_id=to, device_id_type=MESH)
+
+    for e in ORDER[1:AHEAD]:
+        give(e)
+    for e in ORDER[:AHEAD]:
+        start(e)
+    for e in ORDER[AHEAD:]:
+        give(e)
     heads_start()
-    near(0)
-    start(2)
-    start(5)
-    start(7)
-    near(1)
-    far(0)
-    start(6)
-    near(3)
-    far(1)
-    finish(0)
-    near(4)
-    far(3)
-    heads_across()
-    heads_near()
-    finish(1)
-    near(2)
-    far(4)
-    finish(3)
-    near(5)
-    far(2)
-    finish(4)
-    near(7)
-    far(5)
-    heads_far()
-    near(6)
-    finish(2)
-    far(7)
-    finish(5)
-    far(6)
-    finish(7)
-    finish(6)
+    hear(1)
+    for i in range(GROUP):
+        near(ORDER[i])
+        if i + AHEAD < GROUP:
+            start(ORDER[i + AHEAD])
+        if i == HEADS[0]:
+            heads_across()
+            heads_near()
+        if i == HEADS[1]:
+            heads_far()
+        if i >= 2:
+            far(ORDER[i - 2])
+        if i >= 3:
+            finish(ORDER[i - 3])
+        if 3 <= i < 6:
+            hear(i - 1)
+    far(ORDER[6])
+    finish(ORDER[5])
+    far(ORDER[7])
+    finish(ORDER[6])
+    finish(ORDER[7])
 
     def total(line, slots, value, me, count, dev_of, k):
         line[...] = value
@@ -390,6 +397,7 @@
             dma((11,)), dma((11,)),
             dma((NP,)), dma((NP,)),
             dma((3, 2)),
+            pltpu.SemaphoreType.REGULAR((NP // 2 - 1, 2)),
         ],
         compiler_params=pltpu.CompilerParams(
             collective_id=0, has_side_effects=True, vmem_limit_bytes=60 * 1024 * 1024

time: 85.7 us -> 81.5 us (0.951)
  Pallas kernels: 84.1 us -> 79.9 us
    pallas_call x1, Pallas kernels: 84.1 us -> 79.9 us  [shards(): pl.pallas_call(kernel, out_shape=jax.ShapeDtypeStruct((block, lanes), BF1...]
where the time goes in v3:
time: 81.5 us; the launch traced here: 81.3 us
  Pallas kernels  79.9 us (98%)
  local copies, waits for them, and re-layouts  1.38 us (2%)
    pallas_call x1, Pallas kernels, shards(): pl.pallas_call(kernel, out_shape=jax.ShapeDtypeStruct((block, lanes), BF1...  79.9 us

profile of v3, /device:TPU:1, one launch (start us, length us, event | category | flops | bytes accessed | tf_op | source)
XLA Modules:
  0.0 81.3 jit_solution(6077175497317617983)
XLA Ops:
  0.0 79.9 %adasum.1 = bf16[64,256]{1,0:T(8,128)(2,1)} custom-call(bf16[64,4096]{1,0:T(8,128)(2,1)} %g_ref.1, bf16[512,256]{1,0:T(8,128)(2,1)} %a_ref.1), custom_call_target="tpu_custom_call" | custom-call | tf_op jit(solution)/shard_map/adasum/pallas_call | solution.py:375
  79.9 1.4 %copy.4 = bf16[64,256]{1,0:T(8,128)(2,1)} copy(bf16[64,256]{1,0:T(8,128)(2,1)} %adasum.1) | data formatting | bytes 65536

commit v4 on v3

--- a/solution.py
+++ b/solution.py
@@ -14,6 +14,7 @@
 NP = NZ // 2
 GROUP = 2 * NX
 EPS = 1e-6
+VMEM = 55040 * 1024
 ORDER = (0, 1, 3, 4, 5, 7, 2, 6)
 AHEAD = 4
 DIRECT = (0, 6)
@@ -119,19 +120,15 @@
     barrier = pltpu.get_barrier_semaphore()
 
     up, down, over = (y + 1) % NY, (y + NY - 1) % NY, (y + 2) % NY
-    y_up, y_down, core = (dev(x, z, i) for i in (up * 2 + c, down * 2 + c, y * 2 + 1 - c))
+    y_up, y_down, y_over = (dev(x, z, i * 2 + c) for i in (up, down, over))
+    core = dev(x, z, y * 2 + 1 - c)
     z_up, z_down = z_dev((z + 2) % NZ), z_dev((z + NZ - 2) % NZ)
 
     def beside(e):
         return (x + e % NX) % NX, zp * 2 + (zb + e // NX) % 2
 
-    def greet(k, _):
-        to = group_dev((me_group + k) % (GROUP * NT))
-        pl.semaphore_signal(barrier, inc=1, device_id=to, device_id_type=MESH)
-        return 0
-
-    lax.fori_loop(1, GROUP * NT, greet, 0)
-    for to in (z_up, z_down):
+    greeted = [dev(*beside(e), t) for e in ORDER[1:]] + [y_up, y_down, y_over, core, z_up, z_down]
+    for to in greeted:
         pl.semaphore_signal(barrier, inc=1, device_id=to, device_id_type=MESH)
 
     load_g.wait()
@@ -145,7 +142,7 @@
     mine = pl.ds(t * tok, tok)
     gb[0, mine, :] = st[zb * NX + x]
     load_a.wait()
-    pl.semaphore_wait(barrier, GROUP * NT + 1)
+    pl.semaphore_wait(barrier, len(greeted))
 
     sent = []
 
@@ -171,7 +168,7 @@
         spread(e, mine, 1, y_up)
         spread(e, mine, 2, y_down)
         if e in DIRECT:
-            spread(e, mine, 3, dev(x, z, over * 2 + c))
+            spread(e, mine, 3, y_over)
         spread(e, mine, 5, core)
 
     def near(e):
@@ -281,19 +278,23 @@
 
     def hear(step):
         if step > 1:
-            pl.semaphore_wait(heard.at[step - 2, 0], 1)
-            pl.semaphore_wait(heard.at[step - 2, 1], 1)
+            for side in range(5):
+                pl.semaphore_wait(heard.at[step - 2, side], 1)
         if step < NP // 2:
-            for side, to in enumerate((z_up, z_down)):
+            for side, to in enumerate((z_up, z_down, y_up, y_down, core)):
                 pl.semaphore_signal(heard.at[step - 1, side], inc=1, device_id=to, device_id_type=MESH)
 
     for e in ORDER[1:AHEAD]:
         give(e)
-    for e in ORDER[:AHEAD]:
-        start(e)
+    start(0)
+    for copy in sent[:AHEAD - 1]:
+        copy.wait_send()
+    del sent[:AHEAD - 1]
     for e in ORDER[AHEAD:]:
         give(e)
     heads_start()
+    for e in ORDER[1:AHEAD]:
+        start(e)
     hear(1)
     for i in range(GROUP):
         near(ORDER[i])
@@ -397,10 +398,10 @@
             dma((11,)), dma((11,)),
             dma((NP,)), dma((NP,)),
             dma((3, 2)),
-            pltpu.SemaphoreType.REGULAR((NP // 2 - 1, 2)),
+            pltpu.SemaphoreType.REGULAR((NP // 2 - 1, 5)),
         ],
         compiler_params=pltpu.CompilerParams(
-            collective_id=0, has_side_effects=True, vmem_limit_bytes=60 * 1024 * 1024
+            collective_id=0, has_side_effects=True, vmem_limit_bytes=VMEM
         ),
         name="adasum",
     )(grad_out, attn_out)

time: 81.5 us -> 76 us (0.933)
  Pallas kernels: 79.9 us -> 75.2 us
    pallas_call x1, Pallas kernels: 79.9 us -> 75.2 us  [shards(): pl.pallas_call(kernel, out_shape=jax.ShapeDtypeStruct((block, lanes), BF1...]
where the time goes in v4:
time: 76 us; the launch traced here: 75.8 us
  Pallas kernels  75.2 us (99%)
    pallas_call x1, Pallas kernels, shards(): pl.pallas_call(kernel, out_shape=jax.ShapeDtypeStruct((block, lanes), BF1...  75.2 us

profile of v4, /device:TPU:1, one launch (start us, length us, event | category | flops | bytes accessed | tf_op | source)
XLA Modules:
  0.0 75.8 jit_solution(17658207137819047051)
XLA Ops:
  0.0 75.2 %adasum.1 = bf16[64,256]{1,0:T(8,128)(2,1)S(1)} custom-call(bf16[64,4096]{1,0:T(8,128)(2,1)} %g_ref.1, bf16[512,256]{1,0:T(8,128)(2,1)} %a_ref.1), custom_call_target="tpu_custom_call" | custom-call | tf_op jit(solution)/shard_map/adasum/pallas_call | solution.py:376
  75.2 0.6 copy.4

commit v5 on v4

v5 whole, which is shorter than its diff:
```python
import jax
import jax.numpy as jnp
from jax import lax
from jax.experimental import pallas as pl
from jax.experimental.pallas import tpu as pltpu
from jax.sharding import PartitionSpec as P

MESH = pl.DeviceIdType.MESH
F32 = jnp.float32
BF16 = jnp.bfloat16

NX, NY, NZ = 4, 4, 16
NT = 2 * NY
NP = NZ // 2
GROUP = 2 * NX
EPS = 1e-6
VMEM = 55040 * 1024
ORDER = (0, 1, 3, 4, 5, 7, 2, 6)
AHEAD = 4
ROUNDS = 4
DIRECT = (0, 6)
HEADS = (2, 3, 3, 5, 6)
LAG = 3
HEARS = (0, 1, 3, 5)


def sum_rows(value):
    rows, lanes = value.shape
    part = value.reshape(rows // 8, 8, lanes).sum(axis=0)
    return sum(part[:, i : i + 128] for i in range(0, lanes, 128))


def coef(inner, own_sq):
    return 1.0 - inner / (2.0 * (jnp.maximum(own_sq, 0.0) + EPS))


def pack(lines):
    each = jnp.sum(lines, axis=1, keepdims=True)
    row = lax.broadcasted_iota(jnp.int32, lines.shape, 0)
    lane = lax.broadcasted_iota(jnp.int32, lines.shape, 1)
    return jnp.sum(jnp.where(row == lane, each, 0.0), axis=0, keepdims=True)


def tree_weights(line):
    n = 8
    row = lax.broadcasted_iota(jnp.int32, (n, 128), 0)
    lane = lax.broadcasted_iota(jnp.int32, (n, 128), 1)
    col = lane & (n - 1)
    gram = jnp.where(lane // n == row, jnp.broadcast_to(line, (n, 128)), 0.0)
    for shift in (8, 16, 32, 64):
        gram = gram + pltpu.roll(gram, shift, 1)
    first = lane < n
    weight = None
    step = 1
    while step < n:
        diag, pair = col == row, col == (row ^ step)
        c_row = coef(
            jnp.sum(jnp.where(pair & first, gram, 0.0), axis=1, keepdims=True),
            jnp.sum(jnp.where(diag & first, gram, 0.0), axis=1, keepdims=True),
        )
        weight = c_row if weight is None else weight * c_row
        if 2 * step < n:
            c_col = coef(
                jnp.sum(jnp.where(pair, gram, 0.0), axis=0, keepdims=True),
                jnp.sum(jnp.where(diag, gram, 0.0), axis=0, keepdims=True),
            )
            gram = c_row * gram * c_col
            gram = gram + jnp.where(
                (row & step) != 0, pltpu.roll(gram, step, 0), pltpu.roll(gram, n - step, 0)
            )
            gram = gram + jnp.where(
                (col & step) != 0, pltpu.roll(gram, step, 1), pltpu.roll(gram, 128 - step, 1)
            )
        step *= 2
    return weight


def kernel(
    g_ref, a_ref, o_ref,
    gv, st, gb, ab, lbuf, cb, rb, rf, wv, gp1, gp2,
    line1, slots1, line2, slots2, line3, slots3,
    in_sem, gs, gr, as_, ar, zs, zr, sums, heard,
):
    dp, t = lax.axis_index("dp"), lax.axis_index("tensor")
    z, x = dp // NX, dp % NX
    zp, zb = z // 2, z % 2
    y, c = t // 2, t % 2
    tok = g_ref.shape[0]
    block, lanes = o_ref.shape
    part = block // 2

    def dev(xx, zz, tt):
        return (zz * NX + xx, tt)

    def group_dev(i):
        return dev(i // NT % NX, zp * 2 + i // (NT * NX), i % NT)

    def plane_dev(i):
        return dev(i // NT, z, i % NT)

    def z_dev(i):
        return dev(x, i, t)

    me_group, me_plane = (zb * NX + x) * NT + t, x * NT + t

    def send(src, dst, ssem, rsem, to):
        copy = pltpu.make_async_remote_copy(
            src_ref=src, dst_ref=dst, send_sem=ssem, recv_sem=rsem,
            device_id=to, device_id_type=MESH,
        )
        copy.start()
        return copy

    def arrived(dst, rsem):
        pltpu.make_async_copy(dst, dst, rsem).wait()

    load_g = pltpu.make_async_copy(g_ref, gv, in_sem.at[0])
    load_g.start()
    load_a = pltpu.make_async_copy(a_ref, ab.at[0, c], in_sem.at[1])
    load_a.start()

    barrier = pltpu.get_barrier_semaphore()

    up, down, over = (y + 1) % NY, (y + NY - 1) % NY, (y + 2) % NY
    y_up, y_down, y_over = (dev(x, z, i * 2 + c) for i in (up, down, over))
    core = dev(x, z, y * 2 + 1 - c)
    z_up, z_down = z_dev((z + 2) % NZ), z_dev((z + NZ - 2) % NZ)

    def beside(e):
        return (x + e % NX) % NX, zp * 2 + (zb + e // NX) % 2

    greeted = [dev(*beside(e), 2 * y + i) for e in ORDER[1:] for i in range(2)]
    greeted += [y_up, y_down, y_over, core, z_up, z_down]
    for to in greeted:
        pl.semaphore_signal(barrier, inc=1, device_id=to, device_id_type=MESH)

    load_g.wait()
    for i in range(NX):
        for par in range(2):
            for h in range(2):
                for k in range(0, NP, 4):
                    begins = [64 * (NX * (2 * p + par) + i) + 32 * h for p in range(k, k + 4)]
                    st[par * NX + i, h, :, 32 * k : 32 * k + 128] = jnp.concatenate(
                        [gv[:, b : b + 32] for b in begins], axis=1
                    )
    gb[0, pl.ds(t * tok, tok), :] = st[zb * NX + x, c]
    load_a.wait()
    pl.semaphore_wait(barrier, len(greeted))

    sent, owed = [], []

    chip = 2 * tok

    def rows(yy, begin=0, size=chip):
        return pl.ds(yy * chip + begin, size)

    def give(e):
        xx, zz = beside(e)
        back = e // NX * NX + (NX - e % NX) % NX
        mine = pl.ds(t * tok, tok)
        for i in range(2):
            src = st.at[zz % 2 * NX + xx, i]
            to = dev(xx, zz, 2 * y + i)
            sent.append(send(src, gb.at[back, mine], gs.at[e, i], gr.at[back, c], to))

    def give_core():
        src, dst = st.at[zb * NX + x, 1 - c], gb.at[0, pl.ds(t * tok, tok)]
        sent.append(send(src, dst, gs.at[0, 0], gr.at[0, c], core))

    def spread(e, region, k, to):
        ref = gb.at[e, region]
        sent.append(send(ref, ref, gs.at[e, k], gr.at[e, k], to))

    def landed(e, region, k):
        arrived(gb.at[e, region], gr.at[e, k])

    def start(e):
        landed(e, pl.ds((t + 1 - 2 * c) * tok, tok), 1 - c)
        if e:
            landed(e, pl.ds(t * tok, tok), c)
        spread(e, rows(y), 2, y_up)
        spread(e, rows(y), 3, y_down)
        if e in DIRECT:
            spread(e, rows(y), 4, y_over)

    def near(e):
        landed(e, rows(down), 2)
        if e not in DIRECT:
            spread(e, rows(down, 0, tok), 4, y_up)
        landed(e, rows(up), 3)
        if e not in DIRECT:
            spread(e, rows(up, tok, tok), 5, y_down)

    def far(e):
        if e in DIRECT:
            landed(e, rows(over), 4)
        else:
            landed(e, rows(over, 0, tok), 4)
            landed(e, rows(over, tok, tok), 5)

    arows = ab.shape[2] // 2
    low, high, full = pl.ds(0, arows), pl.ds(arows, arows), pl.ds(0, 2 * arows)
    right, left = dev((x + 1) % NX, z, t), dev((x + 3) % NX, z, t)
    across = dev(x, zp * 2 + 1 - zb, t)

    def pass_on(e, to_e, part, k, to):
        sent.append(send(ab.at[e, c, part], ab.at[to_e, c, part], as_.at[k], ar.at[k], to))

    def have(e, part, k, cc=c):
        arrived(ab.at[e, cc, part], ar.at[k])

    def to_core(e):
        for piece, k in heads_needs.get(e, ()):
            have(e, piece, k)
        pass_on(e, e, full, 11 + e, core)

    def heads_start():
        pass_on(0, 4, full, 2, across)
        pass_on(0, 3, low, 0, right)
        pass_on(0, 1, high, 1, left)

    def heads_second():
        pass_on(0, 3, high, 19, right)
        pass_on(0, 1, low, 20, left)
        to_core(0)

    def heads_near():
        have(3, low, 0)
        pass_on(3, 2, low, 3, right)
        have(1, high, 1)
        pass_on(1, 2, high, 4, left)

    def heads_next():
        have(3, high, 19)
        pass_on(3, 7, high, 5, across)
        have(1, low, 20)
        pass_on(1, 5, low, 6, across)
        to_core(3)
        to_core(1)

    quarters = [pl.ds(i * (arows // 2), arows // 2) for i in range(4)]

    def heads_across():
        have(4, full, 2)
        for i in range(2):
            pass_on(4, 7, quarters[i], 7 + 14 * i, right)
            pass_on(4, 5, quarters[3 - i], 8 + 14 * i, left)
        to_core(4)

    def heads_far(i):
        have(7, quarters[i], 7 + 14 * i)
        pass_on(7, 6, quarters[i], 9 + 14 * i, right)
        have(5, quarters[3 - i], 8 + 14 * i)
        pass_on(5, 6, quarters[3 - i], 10 + 14 * i, left)

    heads_needs = {
        2: ((low, 3), (high, 4)),
        5: ((low, 6),),
        7: ((high, 5),),
        6: ((quarters[0], 9), (quarters[1], 23), (quarters[2], 24), (quarters[3], 10)),
    }

    def index(e):
        return (zb + e // NX) % 2 * NX + (x + e % NX) % NX

    def put(gp, i, j, acc):
        line = jnp.sum(acc, axis=0, keepdims=True)
        gp[pl.ds(i * 8 + j, 1), :] = line
        gp[pl.ds(j * 8 + i, 1), :] = line

    def compute(e, before):
        have(e, full, 11 + e, 1 - c)
        r = index(e)
        both = jnp.concatenate([ab[e, 0], ab[e, 1]], axis=1)
        value = lax.dot_general(
            gb[e], both, (((0,), (0,)), ((), ())), preferred_element_type=F32
        )
        lbuf[r] = value
        for o in before:
            put(gp1, r, index(o), sum_rows(value * lbuf[index(o)]))
        put(gp1, r, r, sum_rows(value * value))

    done = []

    def finish(e):
        far(e)
        compute(e, list(done))
        done.append(e)

    def hear(step):
        if step > 1:
            for side in range(5):
                pl.semaphore_wait(heard.at[step - 2, side], 1)
        if step <= ROUNDS:
            for side, to in enumerate((z_up, z_down, y_up, y_down, core)):
                pl.semaphore_signal(heard.at[step - 1, side], inc=1, device_id=to, device_id_type=MESH)

    for e in ORDER[1:AHEAD]:
        give(e)
    firsts = list(sent)
    hear(1)
    sent.clear()
    give_core()
    start(0)
    for copy in firsts:
        copy.wait_send()
    for e in ORDER[AHEAD:]:
        give(e)
    heads_start()
    for e in ORDER[1:AHEAD]:
        start(e)
    heads_second()
    for i in range(GROUP):
        near(ORDER[i])
        if i + AHEAD < GROUP:
            start(ORDER[i + AHEAD])
        if i == HEADS[0]:
            heads_near()
        if i == HEADS[1]:
            heads_across()
        if i == HEADS[2]:
            heads_next()
        if i == HEADS[3]:
            heads_far(0)
        if i == HEADS[4]:
            heads_far(1)
        if i in HEARS:
            hear(HEARS.index(i) + 2)
        if i >= LAG and i < LAG + 4:
            finish(ORDER[i - LAG])
    rest = [e for e in ORDER if e not in done]
    to_core(rest[0])
    to_core(rest[1])
    to_core(rest[2])
    finish(rest[0])
    to_core(rest[3])
    finish(rest[1])
    finish(rest[2])
    finish(rest[3])

    def total(line, slots, value, me, count, dev_of, k):
        line[...] = value
        keep = pltpu.make_async_copy(line, slots.at[pl.ds(me, 1)], sums.at[k, 1])
        keep.start()

        def out(i, _):
            send(line, slots.at[pl.ds(me, 1)], sums.at[k, 0], sums.at[k, 1], dev_of((me + i) % count))
            return 0

        lax.fori_loop(1, count, out, 0)
        every = slots.at[pl.ds(0, count)]
        pltpu.make_async_copy(every, every, sums.at[k, 1]).wait()
        owed.append((slots.at[pl.ds(0, count - 1)], sums.at[k, 0]))
        return jnp.sum(slots[...], axis=0, keepdims=True)

    line = total(line1, slots1, pack(gp1[...]), me_group, GROUP * NT, group_dev, 0)
    wv[...] = jnp.broadcast_to(tree_weights(line), wv.shape)
    w8 = [wv[i : i + 1, :] for i in range(GROUP)]

    def combined(b):
        region = pl.ds(pl.multiple_of(b * part, part), part)
        return sum(w8[i] * lbuf[i, region, :] for i in range(GROUP)).astype(BF16)

    def offer(k, b, i, to):
        sent.append(send(cb.at[b, i], rb.at[zp, c], zs.at[k, i], zr.at[zp, c], to))

    for k in (4, 3, 5, 2, 6, 1, 7, 0):
        b = (zp + k) % NP
        value = combined(b)
        for i in range(2):
            cb[b, i] = value[:, i * lanes : i * lanes + lanes]
        if k:
            for i in range(2):
                offer(k, b, i, dev(x, 2 * b + zb, 2 * y + i))
        else:
            offer(0, b, 1 - c, core)
    rb[zp, c] = cb[zp, c]

    places = []
    for k in (0, 1, 7, 2, 6, 3, 5, 4):
        q = (zp + k) % NP
        arrived(rb.at[q, 1 - c], zr.at[q, 1 - c])
        if k:
            arrived(rb.at[q, c], zr.at[q, c])
        value = rb[q].astype(F32).reshape(block, lanes)
        rf[q] = value
        for o in places:
            put(gp2, q, o, sum_rows(value * rf[o]))
        put(gp2, q, q, sum_rows(value * value))
        places.append(q)

    line = total(line2, slots2, pack(gp2[...]), me_plane, NX * NT, plane_dev, 1)
    line = total(line3, slots3, line, z, NZ, z_dev, 2)
    wv[...] = jnp.broadcast_to(tree_weights(line), wv.shape)
    o_ref[...] = sum(wv[i : i + 1, :lanes] * rf[i] for i in range(NP)).astype(BF16)

    for copy in sent:
        copy.wait_send()
    for others, sem in owed:
        arrived(others, sem)


def shards(grad_out, attn_out):
    tok, width = grad_out.shape
    rows, lanes = attn_out.shape
    wide, block = width // (2 * GROUP), width // (NX * NZ)
    dma, reg = pltpu.SemaphoreType.DMA, pltpu.VMEM
    return pl.pallas_call(
        kernel,
        out_shape=jax.ShapeDtypeStruct((block, lanes), BF16),
        in_specs=[pl.BlockSpec(memory_space=pl.ANY)] * 2,
        out_specs=pl.BlockSpec(memory_space=pltpu.VMEM),
        scratch_shapes=[
            reg((tok, width), BF16),
            reg((GROUP, 2, tok, wide), BF16),
            reg((GROUP, rows, wide), BF16),
            reg((GROUP, 2, rows, lanes), BF16),
            reg((GROUP, wide, 2 * lanes), F32),
            reg((NP, 2, block // 2, lanes), BF16),
            reg((NP, 2, block // 2, lanes), BF16),
            reg((NP, block, lanes), F32),
            reg((8, 2 * lanes), F32),
            reg((64, 128), F32),
            reg((64, 128), F32),
            reg((1, 128), F32), reg((GROUP * NT, 128), F32),
            reg((1, 128), F32), reg((NX * NT, 128), F32),
            reg((1, 128), F32), reg((NZ, 128), F32),
            dma((2,)),
            dma((GROUP, 6)), dma((GROUP, 6)),
            dma((25,)), dma((25,)),
            dma((NP, 2)), dma((NP, 2)),
            dma((3, 2)),
            pltpu.SemaphoreType.REGULAR((ROUNDS, 5)),
        ],
        compiler_params=pltpu.CompilerParams(
            collective_id=0, has_side_effects=True, vmem_limit_bytes=VMEM
        ),
        name="adasum",
    )(grad_out, attn_out)


def solution(mesh):
    return jax.shard_map(
        shards,
        mesh=mesh,
        in_specs=(P(("dp", "tensor"), None), P("dp", "tensor")),
        out_specs=P("dp", "tensor"),
        check_vma=False,
    )
```

time: 76 us -> 74.6 us (0.982)
  Pallas kernels: 75.2 us -> 73.8 us
    pallas_call x1, Pallas kernels: 75.2 us -> 73.8 us  [shards(): pl.pallas_call(kernel, out_shape=jax.ShapeDtypeStruct((block, lanes), BF1...]
where the time goes in v5:
time: 74.6 us; the launch traced here: 74.5 us
  Pallas kernels  73.8 us (99%)
    pallas_call x1, Pallas kernels, shards(): pl.pallas_call(kernel, out_shape=jax.ShapeDtypeStruct((block, lanes), BF1...  73.8 us

profile of v5, /device:TPU:1, one launch (start us, length us, event | category | flops | bytes accessed | tf_op | source)
XLA Modules:
  0.0 74.5 jit_solution(17477831752856479583)
XLA Ops:
  0.0 73.8 %adasum.1 = bf16[64,256]{1,0:T(8,128)(2,1)S(1)} custom-call(bf16[64,4096]{1,0:T(8,128)(2,1)} %g_ref.1, bf16[512,256]{1,0:T(8,128)(2,1)} %a_ref.1), custom_call_target="tpu_custom_call" | custom-call | tf_op jit(solution)/shard_map/adasum/pallas_call | solution.py:408
  73.8 0.6 copy.4

commit v6 on v5

--- a/solution.py
+++ b/solution.py
@@ -307,9 +307,9 @@
     for e in ORDER[AHEAD:]:
         give(e)
     heads_start()
+    heads_second()
     for e in ORDER[1:AHEAD]:
         start(e)
-    heads_second()
     for i in range(GROUP):
         near(ORDER[i])
         if i + AHEAD < GROUP:
@@ -338,6 +338,14 @@
     finish(rest[2])
     finish(rest[3])
 
+    def settle():
+        for copy in sent:
+            copy.wait_send()
+        for others, sem in owed:
+            arrived(others, sem)
+        sent.clear()
+        owed.clear()
+
     def total(line, slots, value, me, count, dev_of, k):
         line[...] = value
         keep = pltpu.make_async_copy(line, slots.at[pl.ds(me, 1)], sums.at[k, 1])
@@ -348,6 +356,7 @@
             return 0
 
         lax.fori_loop(1, count, out, 0)
+        settle()
         every = slots.at[pl.ds(0, count)]
         pltpu.make_async_copy(every, every, sums.at[k, 1]).wait()
         owed.append((slots.at[pl.ds(0, count - 1)], sums.at[k, 0]))
@@ -394,10 +403,7 @@
     wv[...] = jnp.broadcast_to(tree_weights(line), wv.shape)
     o_ref[...] = sum(wv[i : i + 1, :lanes] * rf[i] for i in range(NP)).astype(BF16)
 
-    for copy in sent:
-        copy.wait_send()
-    for others, sem in owed:
-        arrived(others, sem)
+    settle()
 
 
 def shards(grad_out, attn_out):

time: 74.6 us -> 74.5 us (level)
  no operation moved by 1% of the time
where the time goes in v6:
time: 74.5 us; the launch traced here: 74.3 us
  Pallas kernels  73.7 us (99%)
    pallas_call x1, Pallas kernels, shards(): pl.pallas_call(kernel, out_shape=jax.ShapeDtypeStruct((block, lanes), BF1...  73.7 us

profile of v6, /device:TPU:1, one launch (start us, length us, event | category | flops | bytes accessed | tf_op | source)
XLA Modules:
  0.0 74.3 jit_solution(13115549368058742740)
XLA Ops:
  0.0 73.7 %adasum.1 = bf16[64,256]{1,0:T(8,128)(2,1)S(1)} custom-call(bf16[64,4096]{1,0:T(8,128)(2,1)} %g_ref.1, bf16[512,256]{1,0:T(8,128)(2,1)} %a_ref.1), custom_call_target="tpu_custom_call" | custom-call | tf_op jit(solution)/shard_map/adasum/pallas_call | solution.py:414
  73.7 0.6 copy.4
